TPU v7x, 32 devices: a whole 2x2x4 slice. The times are simulated.
32 devices in a mesh: blk: 4 (over y, x), tile: 8 (over z, core).
Axes of the slice: x: 2, y: 2, z: 4, core: 2. Of those that a mesh axis runs over, the one named last changes fastest.
Arguments:
- grid_feat: bfloat16 [8192, 512], P(('blk', 'tile')), may hold values from -18 to 18
- queries: bfloat16 [8192, 512], P(('blk', 'tile')), may hold values from -90 to 90
- obs_keys: bfloat16 [256, 512], P(('blk', 'tile')), may hold values from -4 to 4
- obs_values: bfloat16 [256, 512], P(('blk', 'tile')), may hold values from -6 to 6
- block_mask: int32 [64, 2], P(('blk', 'tile')), may hold values from 0 to 1, as said below
- obs_valid: int32 [2], replicated, may hold values from 2 to 128, as said below
- out_weight: bfloat16 [512, 512], replicated, may hold values from -0.25 to 0.25
- conv_weight: bfloat16 [3, 3, 512, 512], replicated, may hold values from -0.09375 to 0.09375
Outputs:
- layer_out: bfloat16 [8192, 512], P(('blk', 'tile'))
Inputs may be any that keep to these rules, and one draw needn't show every extreme that they name: `block_mask`: row t has a 1 in column t mod 2. `obs_valid`: at least one entry equals 128.
All inputs are finite; a program needn't handle non-finite values.
Results may differ from a plain program's by a relative error of at most 0.007.
Values may be sent and summed in bfloat16 or wider, within the bound.
No kernel may reach another device: no remote copies, remote signals or barrier semaphores. Data moves between devices by JAX's collectives and lax.ppermute only.
A program may use at most 64 MiB of HBM per device.

v0:
```python
import functools
import math

import jax
import jax.numpy as jnp
from jax import lax
from jax.experimental import pallas as pl
from jax.experimental.pallas import tpu as pltpu
from jax.sharding import PartitionSpec as P

HEADS = 8
OBS_BLOCK = 128
AXES = ("blk", "tile")
PAIR = 2
CORES = 2
LIMIT_ROWS = 16


def both_cores(same_ref, other_ref, kind, cols):
    return jnp.concatenate(
        [ref[:, kind, :, cols].reshape(-1, cols.stop - cols.start) for ref in (same_ref, other_ref)],
        axis=0,
    )


def attend(lon, width, nblocks, rows, core, row_refs, keys_of, same_ref, other_ref, weight_refs, mixed_ref):
    head = width // HEADS
    pair = PAIR * head
    obs = nblocks * OBS_BLOCK
    scale = head ** (-0.5) * math.log2(math.e)
    half = OBS_BLOCK // CORES
    key_lane = lax.broadcasted_iota(jnp.int32, (1, OBS_BLOCK), 1)
    spread = (key_lane % half) // rows * (CORES * rows) + key_lane % rows
    first = key_lane < half

    def row_bias(ref):
        limit = ref[2 * lon : 2 * lon + LIMIT_ROWS, :].astype(jnp.float32)[:1].astype(jnp.int32)

        parts = []
        for parity in (core, 1 - core):
            place = spread + parity * rows
            for block in range(0, nblocks, CORES):
                ends = [
                    jnp.broadcast_to(limit[:, b : b + 1], (1, OBS_BLOCK)) for b in (block, block + 1)
                ]
                end = jnp.where(first, ends[0], ends[1])
                parts.append(jnp.where(place < end, 0.0, -jnp.inf))
        return jnp.concatenate(parts, axis=1)

    biases = [row_bias(ref) for ref in row_refs]
    lane = lax.broadcasted_iota(jnp.int32, (obs, pair), 1)
    ones = [(lane // head == h).astype(jnp.bfloat16) for h in range(PAIR)]

    empty = jnp.zeros((head, obs), jnp.bfloat16)

    def columns(group):
        return slice(group * pair, (group + 1) * pair)

    def scores_of(group):
        keys = keys_of(columns(group))
        query = jnp.concatenate([ref[:lon, columns(group)] for ref in row_refs], axis=0)
        scores = []
        for h in range(PAIR):
            part = [keys[i * head : (i + 1) * head] if i == h else empty for i in range(PAIR)]
            part = jnp.concatenate(part, axis=0)
            scores.append(jnp.dot(query, part, preferred_element_type=jnp.float32))
        return scores

    def weights_of(scores):
        pieces = []
        for t, bias in enumerate(biases):
            piece = scores[t * lon : (t + 1) * lon] * scale + bias
            top = jnp.max(piece, axis=1, keepdims=True)
            pieces.append(jnp.exp2(piece - top).astype(jnp.bfloat16))
        return jnp.concatenate(pieces, axis=0)

    groups = HEADS // PAIR
    scores = [scores_of(group) for group in range(groups)]
    weights = [
        jnp.concatenate([weights_of(part) for part in scores[group]], axis=1) for group in range(groups)
    ]
    for group in range(groups):
        values = both_cores(same_ref, other_ref, 1, columns(group))
        value_parts = jnp.concatenate(
            [jnp.concatenate([values * one, one], axis=1) for one in ones], axis=0
        )
        both = jnp.dot(weights[group], value_parts, preferred_element_type=jnp.float32)
        mixed_ref[:, columns(group)] = (both[:, :pair] / both[:, pair:]).astype(jnp.bfloat16)

    depth = width // len(weight_refs)
    projected = sum(
        jnp.dot(
            mixed_ref[:, i * depth : (i + 1) * depth], ref[...], preferred_element_type=jnp.float32
        )
        for i, ref in enumerate(weight_refs)
    )
    grid = jnp.concatenate([ref[lon : 2 * lon, :] for ref in row_refs], axis=0)
    wide = (grid.astype(jnp.float32) + projected).astype(jnp.bfloat16).astype(jnp.float32)
    normed = wide * lax.rsqrt(jnp.mean(wide * wide, axis=-1, keepdims=True) + 1e-06)
    return wide, normed


def around(parts, lon):
    return pltpu.roll(parts[0], 1, 0) + parts[1] + pltpu.roll(parts[2], lon - 1, 0)


def inner_kernel(
    lon, width, nblocks, rows,
    meta_ref, near_ref, near_sent_ref, far_sent_ref, same_ref, other_ref, upper_ref, lower_ref,
    conv_ref, edge_ref, partial_ref, keys_ref, mixed_ref, field_ref,
):
    core = meta_ref[0]

    def keys_of(cols):
        keys = both_cores(same_ref, other_ref, 0, cols).T
        keys_ref[cols, :] = keys
        return keys

    wide, normed = attend(
        lon, width, nblocks, rows, core, (near_ref, near_sent_ref, far_sent_ref), keys_of,
        same_ref, other_ref, (upper_ref, lower_ref), mixed_ref,
    )
    field_ref[...] = normed.astype(jnp.bfloat16)
    edge_ref[...] = field_ref[2 * lon :, :]
    inputs = jnp.concatenate([field_ref[lon:, :], field_ref[: 2 * lon, :]], axis=1)
    terms = []
    for lon_off in range(3):
        taps = jnp.concatenate([conv_ref[1, lon_off], conv_ref[0, lon_off]], axis=0)
        terms.append(jnp.dot(inputs, taps, preferred_element_type=jnp.float32))
    for start in (0, lon):
        here = slice(start, start + lon)
        shifted = around([term[here] for term in terms], lon)
        partial_ref[here, :] = wide[start + lon : start + 2 * lon] + shifted


def outer_kernel(
    lon, width, nblocks, rows,
    meta_ref, far_ref, same_ref, other_ref, upper_ref, lower_ref, edge_ref, partial_ref, keys_ref,
    conv_ref, out_ref, mixed_ref,
):
    core = meta_ref[0]
    _, normed = attend(
        lon, width, nblocks, rows, core, (far_ref,), lambda cols: keys_ref[cols, :],
        same_ref, other_ref, (upper_ref, lower_ref), mixed_ref,
    )
    far = jnp.where(meta_ref[1] > 0, normed, 0.0).astype(jnp.bfloat16)
    field = jnp.concatenate([edge_ref[...], far], axis=0)
    terms = [
        jnp.dot(field, conv_ref[2, lon_off], preferred_element_type=jnp.float32)
        for lon_off in range(3)
    ]
    for start, tile in ((0, 1 - core), (lon, core)):
        here = slice(start, start + lon)
        total = partial_ref[here, :] + around([term[here] for term in terms], lon)
        out_ref[pl.ds(pl.multiple_of(tile * lon, lon), lon), :] = total.astype(jnp.bfloat16)


def pack_kernel(lon, *refs):
    queries_refs, grid_refs, limit_refs = refs[:2], refs[2:4], refs[4:6]
    near_ref, far_ref = refs[6:]
    even = lax.axis_index("tile") % CORES == 0
    for place, pair_refs in (
        (slice(0, lon), queries_refs),
        (slice(lon, 2 * lon), grid_refs),
        (slice(2 * lon, 2 * lon + LIMIT_ROWS), limit_refs),
    ):
        first, last = pair_refs[0][...], pair_refs[1][...]
        far_ref[place, :] = jnp.where(even, first, last)
        near_ref[place, :] = jnp.where(even, last, first)


def fetch_kernel(conv_hbm, conv_ref, sems):
    core = lax.axis_index("tile") % CORES
    copies = [
        pltpu.make_async_copy(conv_hbm.at[source], conv_ref.at[i], sems.at[i])
        for i, source in enumerate((2 - 2 * core, 1, 2 * core))
    ]
    for copy in copies:
        copy.start()
    for copy in copies:
        copy.wait()


def on_device(
    grid_feat, queries, obs_keys, obs_values, block_mask, obs_valid, out_weight, conv_weight
):
    q_dev, width = queries.shape
    tiles, nblocks = block_mask.shape
    rows = obs_keys.shape[0]
    lon = q_dev // tiles
    obs = nblocks * OBS_BLOCK
    devices = lax.axis_size(AXES)
    pairs = devices // CORES
    me = lax.axis_index(AXES)
    core = me % CORES

    block = jnp.stack([obs_keys, obs_values])
    groups = [list(range(c, devices, CORES)) for c in range(CORES)]
    same = lax.all_to_all(
        jnp.broadcast_to(block[None], (pairs,) + block.shape), AXES, 0, 0, axis_index_groups=groups
    )
    swap = [(i, i ^ 1) for i in range(devices)]
    across = [(i, i + 1) for i in range(1, devices - 1, CORES)]
    across += [(target, source) for source, target in across]

    query_rows, grid_rows = lax.optimization_barrier(
        (jnp.split(queries, tiles, axis=0), jnp.split(grid_feat, tiles, axis=0))
    )
    limits = jnp.where(block_mask > 0, obs_valid[None], 0).astype(jnp.bfloat16)
    limits = jnp.pad(limits, ((0, 0), (0, width - nblocks)))

    limit_rows = [
        jnp.broadcast_to(limits[tile][None], (LIMIT_ROWS, width)) for tile in range(tiles)
    ]
    vmem = pl.BlockSpec(memory_space=pltpu.VMEM)
    payload = jax.ShapeDtypeStruct((2 * lon + LIMIT_ROWS, width), jnp.bfloat16)
    near_sent, far_sent = pl.pallas_call(
        functools.partial(pack_kernel, lon),
        out_shape=[payload] * 2,
        in_specs=[vmem] * 6,
        out_specs=[vmem] * 2,
        compiler_params=pltpu.CompilerParams(vmem_limit_bytes=4 * 2**20),
        cost_estimate=pl.CostEstimate(flops=10**10, bytes_accessed=8 * payload.size, transcendentals=0),
        name="pack",
    )(*query_rows, *grid_rows, *limit_rows)
    far = lax.ppermute(far_sent, AXES, across)
    near = lax.ppermute(near_sent, AXES, swap)
    conv_weight, _ = lax.optimization_barrier((conv_weight, near_sent))
    taps = pl.pallas_call(
        fetch_kernel,
        out_shape=jax.ShapeDtypeStruct(conv_weight.shape, jnp.bfloat16),
        in_specs=[pl.BlockSpec(memory_space=pltpu.HBM)],
        out_specs=vmem,
        scratch_shapes=[pltpu.SemaphoreType.DMA((3,))],
        compiler_params=pltpu.CompilerParams(vmem_limit_bytes=4 * 2**20),
        cost_estimate=pl.CostEstimate(flops=0, bytes_accessed=4 * conv_weight.size, transcendentals=0),
        name="fetch",
    )(conv_weight)
    same, taps = lax.optimization_barrier((same, taps))
    other = lax.ppermute(same, AXES, swap)
    out_weight, _ = lax.optimization_barrier((out_weight, same))
    upper, lower = lax.optimization_barrier(tuple(jnp.split(out_weight, 2, axis=0)))

    far_exists = (me > 0) & (me < devices - 1)
    meta = jnp.stack([core, far_exists.astype(core.dtype)]).astype(jnp.int32)

    smem = pl.BlockSpec(memory_space=pltpu.SMEM)
    sizes = (lon, width, nblocks, rows)
    params = pltpu.CompilerParams(vmem_limit_bytes=40 * 2**20)
    tap_flops, row_flops = 2 * lon * width * width, 2 * lon * width * (width + 4 * obs)
    edge, partial, keys = pl.pallas_call(
        functools.partial(inner_kernel, *sizes),
        out_shape=[
            jax.ShapeDtypeStruct((lon, width), jnp.bfloat16),
            jax.ShapeDtypeStruct((q_dev, width), jnp.float32),
            jax.ShapeDtypeStruct((width, obs), jnp.bfloat16),
        ],
        in_specs=[smem] + [vmem] * 8,
        out_specs=[vmem] * 3,
        scratch_shapes=[
            pltpu.VMEM((3 * lon, width), jnp.bfloat16),
            pltpu.VMEM((3 * lon, width), jnp.bfloat16),
        ],
        compiler_params=params,
        cost_estimate=pl.CostEstimate(
            flops=3 * row_flops + 12 * tap_flops, bytes_accessed=2 * conv_weight.size, transcendentals=0
        ),
        name="inner",
    )(meta, near, near_sent, far_sent, same, other, upper, lower, taps)
    return pl.pallas_call(
        functools.partial(outer_kernel, *sizes),
        out_shape=jax.ShapeDtypeStruct((q_dev, width), jnp.bfloat16),
        in_specs=[smem] + [vmem] * 9,
        out_specs=vmem,
        scratch_shapes=[
            pltpu.VMEM((lon, width), jnp.bfloat16),
        ],
        compiler_params=params,
        cost_estimate=pl.CostEstimate(
            flops=row_flops + 6 * tap_flops, bytes_accessed=conv_weight.size, transcendentals=0
        ),
        name="outer",
    )(meta, far, same, other, upper, lower, edge, partial, keys, taps)


def solution(mesh):
    in_specs = (
        P(AXES, None),
        P(AXES, None),
        P(AXES, None),
        P(AXES, None),
        P(AXES, None),
        P(),
        P(),
        P(),
    )
    return jax.shard_map(
        on_device, mesh=mesh, in_specs=in_specs, out_specs=P(AXES, None), check_vma=False
    )
```

profile of v0, /device:TPU:5, one launch (start us, length us, event | category | flops | bytes accessed | tf_op | source)
XLA Modules:
  0.0 31.8 jit_solution(11751223216927017468)
XLA Ops:
  0.0 0.7 %pad_maximum_fusion = bf16[2,8,512]{2,1,0:T(8,128)(2,1)S(1)} fusion(bf16[1,8,512]{2,1,0:T(8,128)(2,1)} %bitcast.4, bf16[1,8,512]{2,1,0:T(8,128)(2,1)} %bitcast.5), kind=kLoop, calls=%fused_computation | loop fusion | flops 8192 | bytes 32768 | tf_op jit(solution)/shard_map/stack | solution.py:197
  0.7 0.7 %broadcast_in_dim.36 = bf16[16,2,8,512]{3,2,1,0:T(8,128)(2,1)} broadcast(bf16[2,8,512]{2,1,0:T(8,128)(2,1)S(1)} %pad_maximum_fusion), dimensions={1,2,3} | broadcast | bytes 278528 | tf_op jit(solution)/shard_map/broadcast_in_dim | solution.py:200
  1.4 6.7 %all-to-all-start = ((bf16[16,2,8,512]{3,2,1,0:T(8,128)(2,1)}), bf16[16,2,8,512]{3,2,1,0:T(8,128)(2,1)S(1)}, u32[]{:S(2)}, u32[]{:S(2)}) async-start(bf16[16,2,8,512]{3,2,1,0:T(8,128)(2,1)} %broadcast_in_dim.36), calls=%async_computation | async-start | bytes 524288 | tf_op jit(solution)/shard_map/all_to_all | solution.py:199
  8.2 1.1 %fusion.2 = (bf16[128,512]{1,0:T(8,128)(2,1)S(1)}, bf16[128,512]{1,0:T(8,128)(2,1)S(1)}, bf16[128,512]{1,0:T(8,128)(2,1)S(1)}, bf16[128,512]{1,0:T(8,128)(2,1)S(1)}) fusion(bf16[256,512]{1,0:T(8,128)(2,1)} %param.8, bf16[256,512]{1,0:T(8,128)(2,1)} %param.9), kind=kLoop, calls=%fused_computation.7 | loop fusion | bytes 1048576 | tf_op jit(solution)/shard_map/split | solution.py:207
  9.3 0.7 %fusion = bf16[2,2]{1,0:T(2,128)(2,1)S(1)} fusion(s32[2,2]{1,0:T(2,128)} %param.12, s32[2]{0:T(128)} %param.13), kind=kLoop, calls=%fused_computation.4 | loop fusion | flops 12 | bytes 32 | tf_op jit(solution)/shard_map/convert_element_type | solution.py:209
  10.0 0.1 pack.1
  10.1 1.3 %collective-permute-start.2 = (bf16[272,512]{1,0:T(8,128)(2,1)S(1)}, bf16[272,512]{1,0:T(8,128)(2,1)S(1)}, u32[]{:S(2)}, u32[]{:S(2)}) collective-permute-start(bf16[272,512]{1,0:T(8,128)(2,1)S(1)} %get-tuple-element.25.near_sent_ref), channel_id=1, source_target_pairs={{0,1},{1,0},{2,3},{3,2},{4,5},{5,4},{6,7},{7,6},{8,9},{9,8},{10,11... | collective-permute-start | bytes 835592 | tf_op jit(solution)/shard_map/ppermute | solution.py:227
  11.4 3.0 %collective-permute-start = (bf16[272,512]{1,0:T(8,128)(2,1)S(1)}, bf16[272,512]{1,0:T(8,128)(2,1)S(1)}, u32[]{:S(2)}, u32[]{:S(2)}) collective-permute-start(bf16[272,512]{1,0:T(8,128)(2,1)S(1)} %get-tuple-element.24.far_sent_ref), channel_id=1, source_target_pairs={{1,2},{3,4},{5,6},{7,8},{9,10},{11,12},{13,14},{15,16},{17,18},{19... | collective-permute-start | bytes 835592 | tf_op jit(solution)/shard_map/ppermute | solution.py:226
  14.4 0.0 copy-start.3
  14.4 2.3 %copy-done.3 = bf16[3,3,512,512]{3,2,1,0:T(8,128)(2,1)S(1)} copy-done((bf16[3,3,512,512]{3,2,1,0:T(8,128)(2,1)S(1)}, bf16[3,3,512,512]{3,2,1,0:T(8,128)(2,1)}, u32[]{:S(2)}) %copy-start.3) | copy-done | bytes 4718616
  16.8 0.3 %fetch.1.conv_ref = bf16[3,3,512,512]{3,2,1,0:T(8,128)(2,1)S(1)} custom-call(bf16[3,3,512,512]{3,2,1,0:T(8,128)(2,1)S(1)} %copy-done.3), custom_call_target="tpu_custom_call" | custom-call | bytes 9437184 | tf_op jit(solution)/shard_map/fetch/pallas_call | solution.py:229
  17.1 0.0 copy-start
  17.1 2.1 %copy-done = bf16[3,3,512,512]{3,2,1,0:T(8,128)(2,1)} copy-done((bf16[3,3,512,512]{3,2,1,0:T(8,128)(2,1)}, bf16[3,3,512,512]{3,2,1,0:T(8,128)(2,1)S(1)}, u32[]{:S(2)}) %copy-start) | copy-done | bytes 4718616
  19.2 0.0 all-to-all-done.same_ref
  19.2 3.2 %collective-permute-start.1 = (bf16[16,2,8,512]{3,2,1,0:T(8,128)(2,1)S(1)}, bf16[16,2,8,512]{3,2,1,0:T(8,128)(2,1)S(1)}, u32[]{:S(2)}, u32[]{:S(2)}) collective-permute-start(bf16[16,2,8,512]{3,2,1,0:T(8,128)(2,1)S(1)} %all-to-all-done.same_ref), channel_id=1, source_target_pairs={{0,1},{1,0},{2,3},{3,2},{4,5},{5,4},{6,7},{7,6},{8,9},{9,8},{10,11... | collective-permute-start | bytes 786440 | tf_op jit(solution)/shard_map/ppermute | solution.py:240
  22.4 0.1 pad_add_fusion.meta_ref
  22.5 0.0 copy-done.4
  22.5 0.0 collective-permute-done.2.near_ref
  22.6 1.0 %collective-permute-done.1.other_ref = bf16[16,2,8,512]{3,2,1,0:T(8,128)(2,1)S(1)} collective-permute-done((bf16[16,2,8,512]{3,2,1,0:T(8,128)(2,1)S(1)}, bf16[16,2,8,512]{3,2,1,0:T(8,128)(2,1)S(1)}, u32[]{:S(2)}, u32[]{:S(2)}) %collective-permute-start.1) | collective-permute-done | bytes 262176 | tf_op jit(solution)/shard_map/ppermute | solution.py:240
  23.6 2.3 %copy-done.1 = bf16[3,3,512,512]{3,2,1,0:T(8,128)(2,1)S(1)} copy-done((bf16[3,3,512,512]{3,2,1,0:T(8,128)(2,1)S(1)}, bf16[3,3,512,512]{3,2,1,0:T(8,128)(2,1)}, u32[]{:S(2)}) %copy-start.1) | copy-done | bytes 4718616
  25.9 3.2 %inner.1 = (bf16[128,512]{1,0:T(8,128)(2,1)S(1)}, f32[256,512]{1,0:T(8,128)S(1)}, bf16[512,256]{1,0:T(8,128)(2,1)S(1)}) custom-call(s32[2]{0:T(128)S(1)} %pad_add_fusion.meta_ref, bf16[272,512]{1,0:T(8,128)(2,1)S(1)} %collective-permute-done.2.near_ref, bf16[272,512]{1,0:T(8,128)(2,1)S(1)} %get-tuple-element.25.near_sent_ref, ...), custom_call_target="tpu_custom_call" | custom-call | flops 1409286144 | bytes 4718592 | tf_op jit(solution)/shard_map/inner/pallas_call | solution.py:251
  29.1 0.0 collective-permute-done.far_ref
  29.1 0.0 copy-done.2
  29.1 2.6 %outer.1 = bf16[256,512]{1,0:T(8,128)(2,1)} custom-call(s32[2]{0:T(128)S(1)} %pad_add_fusion.meta_ref, bf16[272,512]{1,0:T(8,128)(2,1)S(1)} %collective-permute-done.far_ref, bf16[16,2,8,512]{3,2,1,0:T(8,128)(2,1)S(1)} %all-to-all-done.same_ref, bf16[16,2,8,512]{3,2,1,0:T(8,128)(2,1)S(1)} %collective-permute-done.1.other_ref, ...), custom_call_target="tpu_custom_call" | custom-call | flops 603979776 | bytes 2359296 | tf_op jit(solution)/shard_map/outer/pallas_call | solution.py:270
  (7 shorter events, 0.1 us)
Async XLA Ops:
  1.4 17.8 %all-to-all-start = ((bf16[16,2,8,512]{3,2,1,0:T(8,128)(2,1)}), bf16[16,2,8,512]{3,2,1,0:T(8,128)(2,1)S(1)}, u32[]{:S(2)}, u32[]{:S(2)}) async-start(bf16[16,2,8,512]{3,2,1,0:T(8,128)(2,1)} %broadcast_in_dim.36), calls=%async_computation | async-start | bytes 524288 | tf_op jit(solution)/shard_map/all_to_all | solution.py:199
  10.1 12.4 %collective-permute-start.2 = (bf16[272,512]{1,0:T(8,128)(2,1)S(1)}, bf16[272,512]{1,0:T(8,128)(2,1)S(1)}, u32[]{:S(2)}, u32[]{:S(2)}) collective-permute-start(bf16[272,512]{1,0:T(8,128)(2,1)S(1)} %get-tuple-element.25.near_sent_ref), channel_id=1, source_target_pairs={{0,1},{1,0},{2,3},{3,2},{4,5},{5,4},{6,7},{7,6},{8,9},{9,8},{10,11... | collective-permute-start | bytes 835592 | tf_op jit(solution)/shard_map/ppermute | solution.py:227
  11.4 17.7 %collective-permute-start = (bf16[272,512]{1,0:T(8,128)(2,1)S(1)}, bf16[272,512]{1,0:T(8,128)(2,1)S(1)}, u32[]{:S(2)}, u32[]{:S(2)}) collective-permute-start(bf16[272,512]{1,0:T(8,128)(2,1)S(1)} %get-tuple-element.24.far_sent_ref), channel_id=1, source_target_pairs={{1,2},{3,4},{5,6},{7,8},{9,10},{11,12},{13,14},{15,16},{17,18},{19... | collective-permute-start | bytes 835592 | tf_op jit(solution)/shard_map/ppermute | solution.py:226
  14.4 2.3 %copy-start.3 = (bf16[3,3,512,512]{3,2,1,0:T(8,128)(2,1)S(1)}, bf16[3,3,512,512]{3,2,1,0:T(8,128)(2,1)}, u32[]{:S(2)}) copy-start(bf16[3,3,512,512]{3,2,1,0:T(8,128)(2,1)} %conv_hbm) | copy-start | bytes 14155780
  16.8 5.7 %copy-start.4 = (bf16[512,512]{1,0:T(8,128)(2,1)S(1)}, bf16[512,512]{1,0:T(8,128)(2,1)}, u32[]{:S(2)}) copy-start(bf16[512,512]{1,0:T(8,128)(2,1)} %param.14) | copy-start | bytes 1572868
  17.1 2.1 %copy-start = (bf16[3,3,512,512]{3,2,1,0:T(8,128)(2,1)}, bf16[3,3,512,512]{3,2,1,0:T(8,128)(2,1)S(1)}, u32[]{:S(2)}) copy-start(bf16[3,3,512,512]{3,2,1,0:T(8,128)(2,1)S(1)} %fetch.1.conv_ref) | copy-start | bytes 14155780
  19.2 4.3 %collective-permute-start.1 = (bf16[16,2,8,512]{3,2,1,0:T(8,128)(2,1)S(1)}, bf16[16,2,8,512]{3,2,1,0:T(8,128)(2,1)S(1)}, u32[]{:S(2)}, u32[]{:S(2)}) collective-permute-start(bf16[16,2,8,512]{3,2,1,0:T(8,128)(2,1)S(1)} %all-to-all-done.same_ref), channel_id=1, source_target_pairs={{0,1},{1,0},{2,3},{3,2},{4,5},{5,4},{6,7},{7,6},{8,9},{9,8},{10,11... | collective-permute-start | bytes 786440 | tf_op jit(solution)/shard_map/ppermute | solution.py:240
  23.6 2.3 %copy-start.1 = (bf16[3,3,512,512]{3,2,1,0:T(8,128)(2,1)S(1)}, bf16[3,3,512,512]{3,2,1,0:T(8,128)(2,1)}, u32[]{:S(2)}) copy-start(bf16[3,3,512,512]{3,2,1,0:T(8,128)(2,1)} %copy-done) | copy-start | bytes 14155780
  25.9 3.2 %copy-start.2 = (bf16[3,3,512,512]{3,2,1,0:T(8,128)(2,1)S(1)}, bf16[3,3,512,512]{3,2,1,0:T(8,128)(2,1)}, u32[]{:S(2)}) copy-start(bf16[3,3,512,512]{3,2,1,0:T(8,128)(2,1)} %copy-done) | copy-start | bytes 14155780
where the time goes:
time: 32.2 us; the launch traced here: 31.8 us
  starting transfers between devices  14.2 us (44%)
  local copies, waits for them, and re-layouts  8.73 us (27%)
  Pallas kernels  6.2 us (19%)
  other arithmetic  1.48 us (5%)
  waiting for transfers between devices  1.04 us (3%)
    unnamed x10, local copies, waits for them, and re-layouts  6.8 us
    all_to_all x1, starting transfers between devices, on_device(): lax.all_to_all(jnp.broadcast_to(block[None], (pairs,) + block.shape), AXE...  6.72 us
    ppermute x1, starting transfers between devices, on_device(): other = lax.ppermute(same, AXES, swap)  3.18 us
    pallas_call x1, Pallas kernels, on_device(): pl.pallas_call(functools.partial(inner_kernel, *sizes), out_shape=[jax.Sh...  3.17 us
    ppermute x1, starting transfers between devices, on_device(): far = lax.ppermute(far_sent, AXES, across)  2.99 us
    pallas_call x1, Pallas kernels, on_device(): pl.pallas_call(functools.partial(outer_kernel, *sizes), out_shape=jax.Sha...  2.64 us
    ppermute x1, starting transfers between devices, on_device(): near = lax.ppermute(near_sent, AXES, swap)  1.3 us
    split x1, local copies, waits for them, and re-layouts, on_device(): jnp.split(grid_feat, tiles, axis=0)  1.13 us
  transfers between devices with their start and end apart: 4, of which 1 were waited for; matrix products, arithmetic and copies ran while one was open for 6% of the time, Pallas kernels for 11%

commit v1 on v0

--- a/solution.py
+++ b/solution.py
@@ -246,7 +246,7 @@
 
     smem = pl.BlockSpec(memory_space=pltpu.SMEM)
     sizes = (lon, width, nblocks, rows)
-    params = pltpu.CompilerParams(vmem_limit_bytes=40 * 2**20)
+    params = pltpu.CompilerParams(vmem_limit_bytes=(16 + 2 * nblocks) * 2**20)
     tap_flops, row_flops = 2 * lon * width * width, 2 * lon * width * (width + 4 * obs)
     edge, partial, keys = pl.pallas_call(
         functools.partial(inner_kernel, *sizes),

time: 32.2 us -> 32.2 us (level)
  no operation moved by 1% of the time
where the time goes in v1:
time: 32.2 us; the launch traced here: 31.8 us
  starting transfers between devices  14.2 us (44%)
  local copies, waits for them, and re-layouts  8.73 us (27%)
  Pallas kernels  6.2 us (19%)
  other arithmetic  1.48 us (5%)
  waiting for transfers between devices  1.04 us (3%)
    unnamed x10, local copies, waits for them, and re-layouts  6.8 us
    all_to_all x1, starting transfers between devices, on_device(): lax.all_to_all(jnp.broadcast_to(block[None], (pairs,) + block.shape), AXE...  6.72 us
    ppermute x1, starting transfers between devices, on_device(): other = lax.ppermute(same, AXES, swap)  3.18 us
    pallas_call x1, Pallas kernels, on_device(): pl.pallas_call(functools.partial(inner_kernel, *sizes), out_shape=[jax.Sh...  3.17 us
    ppermute x1, starting transfers between devices, on_device(): far = lax.ppermute(far_sent, AXES, across)  2.99 us
    pallas_call x1, Pallas kernels, on_device(): pl.pallas_call(functools.partial(outer_kernel, *sizes), out_shape=jax.Sha...  2.64 us
    ppermute x1, starting transfers between devices, on_device(): near = lax.ppermute(near_sent, AXES, swap)  1.3 us
    split x1, local copies, waits for them, and re-layouts, on_device(): jnp.split(grid_feat, tiles, axis=0)  1.13 us
  transfers between devices with their start and end apart: 4, of which 1 were waited for; matrix products, arithmetic and copies ran while one was open for 6% of the time, Pallas kernels for 11%

profile of v1, /device:TPU:5, one launch (start us, length us, event | category | flops | bytes accessed | tf_op | source)
XLA Modules:
  0.0 31.8 jit_solution(3272503632905399396)
XLA Ops:
  0.0 0.7 %pad_maximum_fusion = bf16[2,8,512]{2,1,0:T(8,128)(2,1)S(1)} fusion(bf16[1,8,512]{2,1,0:T(8,128)(2,1)} %bitcast.4, bf16[1,8,512]{2,1,0:T(8,128)(2,1)} %bitcast.5), kind=kLoop, calls=%fused_computation | loop fusion | flops 8192 | bytes 32768 | tf_op jit(solution)/shard_map/stack | solution.py:197
  0.7 0.7 %broadcast_in_dim.36 = bf16[16,2,8,512]{3,2,1,0:T(8,128)(2,1)} broadcast(bf16[2,8,512]{2,1,0:T(8,128)(2,1)S(1)} %pad_maximum_fusion), dimensions={1,2,3} | broadcast | bytes 278528 | tf_op jit(solution)/shard_map/broadcast_in_dim | solution.py:200
  1.4 6.7 %all-to-all-start = ((bf16[16,2,8,512]{3,2,1,0:T(8,128)(2,1)}), bf16[16,2,8,512]{3,2,1,0:T(8,128)(2,1)S(1)}, u32[]{:S(2)}, u32[]{:S(2)}) async-start(bf16[16,2,8,512]{3,2,1,0:T(8,128)(2,1)} %broadcast_in_dim.36), calls=%async_computation | async-start | bytes 524288 | tf_op jit(solution)/shard_map/all_to_all | solution.py:199
  8.2 1.1 %fusion.2 = (bf16[128,512]{1,0:T(8,128)(2,1)S(1)}, bf16[128,512]{1,0:T(8,128)(2,1)S(1)}, bf16[128,512]{1,0:T(8,128)(2,1)S(1)}, bf16[128,512]{1,0:T(8,128)(2,1)S(1)}) fusion(bf16[256,512]{1,0:T(8,128)(2,1)} %param.8, bf16[256,512]{1,0:T(8,128)(2,1)} %param.9), kind=kLoop, calls=%fused_computation.7 | loop fusion | bytes 1048576 | tf_op jit(solution)/shard_map/split | solution.py:207
  9.3 0.7 %fusion = bf16[2,2]{1,0:T(2,128)(2,1)S(1)} fusion(s32[2,2]{1,0:T(2,128)} %param.12, s32[2]{0:T(128)} %param.13), kind=kLoop, calls=%fused_computation.4 | loop fusion | flops 12 | bytes 32 | tf_op jit(solution)/shard_map/convert_element_type | solution.py:209
  10.0 0.1 pack.1
  10.1 1.3 %collective-permute-start.2 = (bf16[272,512]{1,0:T(8,128)(2,1)S(1)}, bf16[272,512]{1,0:T(8,128)(2,1)S(1)}, u32[]{:S(2)}, u32[]{:S(2)}) collective-permute-start(bf16[272,512]{1,0:T(8,128)(2,1)S(1)} %get-tuple-element.25.near_sent_ref), channel_id=1, source_target_pairs={{0,1},{1,0},{2,3},{3,2},{4,5},{5,4},{6,7},{7,6},{8,9},{9,8},{10,11... | collective-permute-start | bytes 835592 | tf_op jit(solution)/shard_map/ppermute | solution.py:227
  11.4 3.0 %collective-permute-start = (bf16[272,512]{1,0:T(8,128)(2,1)S(1)}, bf16[272,512]{1,0:T(8,128)(2,1)S(1)}, u32[]{:S(2)}, u32[]{:S(2)}) collective-permute-start(bf16[272,512]{1,0:T(8,128)(2,1)S(1)} %get-tuple-element.24.far_sent_ref), channel_id=1, source_target_pairs={{1,2},{3,4},{5,6},{7,8},{9,10},{11,12},{13,14},{15,16},{17,18},{19... | collective-permute-start | bytes 835592 | tf_op jit(solution)/shard_map/ppermute | solution.py:226
  14.4 0.0 copy-start.3
  14.4 2.3 %copy-done.3 = bf16[3,3,512,512]{3,2,1,0:T(8,128)(2,1)S(1)} copy-done((bf16[3,3,512,512]{3,2,1,0:T(8,128)(2,1)S(1)}, bf16[3,3,512,512]{3,2,1,0:T(8,128)(2,1)}, u32[]{:S(2)}) %copy-start.3) | copy-done | bytes 4718616
  16.8 0.3 %fetch.1.conv_ref = bf16[3,3,512,512]{3,2,1,0:T(8,128)(2,1)S(1)} custom-call(bf16[3,3,512,512]{3,2,1,0:T(8,128)(2,1)S(1)} %copy-done.3), custom_call_target="tpu_custom_call" | custom-call | bytes 9437184 | tf_op jit(solution)/shard_map/fetch/pallas_call | solution.py:229
  17.1 0.0 copy-start
  17.1 2.1 %copy-done = bf16[3,3,512,512]{3,2,1,0:T(8,128)(2,1)} copy-done((bf16[3,3,512,512]{3,2,1,0:T(8,128)(2,1)}, bf16[3,3,512,512]{3,2,1,0:T(8,128)(2,1)S(1)}, u32[]{:S(2)}) %copy-start) | copy-done | bytes 4718616
  19.2 0.0 all-to-all-done.same_ref
  19.2 3.2 %collective-permute-start.1 = (bf16[16,2,8,512]{3,2,1,0:T(8,128)(2,1)S(1)}, bf16[16,2,8,512]{3,2,1,0:T(8,128)(2,1)S(1)}, u32[]{:S(2)}, u32[]{:S(2)}) collective-permute-start(bf16[16,2,8,512]{3,2,1,0:T(8,128)(2,1)S(1)} %all-to-all-done.same_ref), channel_id=1, source_target_pairs={{0,1},{1,0},{2,3},{3,2},{4,5},{5,4},{6,7},{7,6},{8,9},{9,8},{10,11... | collective-permute-start | bytes 786440 | tf_op jit(solution)/shard_map/ppermute | solution.py:240
  22.4 0.1 pad_add_fusion.meta_ref
  22.5 0.0 copy-done.4
  22.5 0.0 collective-permute-done.2.near_ref
  22.6 1.0 %collective-permute-done.1.other_ref = bf16[16,2,8,512]{3,2,1,0:T(8,128)(2,1)S(1)} collective-permute-done((bf16[16,2,8,512]{3,2,1,0:T(8,128)(2,1)S(1)}, bf16[16,2,8,512]{3,2,1,0:T(8,128)(2,1)S(1)}, u32[]{:S(2)}, u32[]{:S(2)}) %collective-permute-start.1) | collective-permute-done | bytes 262176 | tf_op jit(solution)/shard_map/ppermute | solution.py:240
  23.6 2.3 %copy-done.1 = bf16[3,3,512,512]{3,2,1,0:T(8,128)(2,1)S(1)} copy-done((bf16[3,3,512,512]{3,2,1,0:T(8,128)(2,1)S(1)}, bf16[3,3,512,512]{3,2,1,0:T(8,128)(2,1)}, u32[]{:S(2)}) %copy-start.1) | copy-done | bytes 4718616
  25.9 3.2 %inner.1 = (bf16[128,512]{1,0:T(8,128)(2,1)S(1)}, f32[256,512]{1,0:T(8,128)S(1)}, bf16[512,256]{1,0:T(8,128)(2,1)S(1)}) custom-call(s32[2]{0:T(128)S(1)} %pad_add_fusion.meta_ref, bf16[272,512]{1,0:T(8,128)(2,1)S(1)} %collective-permute-done.2.near_ref, bf16[272,512]{1,0:T(8,128)(2,1)S(1)} %get-tuple-element.25.near_sent_ref, ...), custom_call_target="tpu_custom_call" | custom-call | flops 1409286144 | bytes 4718592 | tf_op jit(solution)/shard_map/inner/pallas_call | solution.py:251
  29.1 0.0 collective-permute-done.far_ref
  29.1 0.0 copy-done.2
  29.1 2.6 %outer.1 = bf16[256,512]{1,0:T(8,128)(2,1)} custom-call(s32[2]{0:T(128)S(1)} %pad_add_fusion.meta_ref, bf16[272,512]{1,0:T(8,128)(2,1)S(1)} %collective-permute-done.far_ref, bf16[16,2,8,512]{3,2,1,0:T(8,128)(2,1)S(1)} %all-to-all-done.same_ref, bf16[16,2,8,512]{3,2,1,0:T(8,128)(2,1)S(1)} %collective-permute-done.1.other_ref, ...), custom_call_target="tpu_custom_call" | custom-call | flops 603979776 | bytes 2359296 | tf_op jit(solution)/shard_map/outer/pallas_call | solution.py:270
  (7 shorter events, 0.1 us)
Async XLA Ops:
  1.4 17.8 %all-to-all-start = ((bf16[16,2,8,512]{3,2,1,0:T(8,128)(2,1)}), bf16[16,2,8,512]{3,2,1,0:T(8,128)(2,1)S(1)}, u32[]{:S(2)}, u32[]{:S(2)}) async-start(bf16[16,2,8,512]{3,2,1,0:T(8,128)(2,1)} %broadcast_in_dim.36), calls=%async_computation | async-start | bytes 524288 | tf_op jit(solution)/shard_map/all_to_all | solution.py:199
  10.1 12.4 %collective-permute-start.2 = (bf16[272,512]{1,0:T(8,128)(2,1)S(1)}, bf16[272,512]{1,0:T(8,128)(2,1)S(1)}, u32[]{:S(2)}, u32[]{:S(2)}) collective-permute-start(bf16[272,512]{1,0:T(8,128)(2,1)S(1)} %get-tuple-element.25.near_sent_ref), channel_id=1, source_target_pairs={{0,1},{1,0},{2,3},{3,2},{4,5},{5,4},{6,7},{7,6},{8,9},{9,8},{10,11... | collective-permute-start | bytes 835592 | tf_op jit(solution)/shard_map/ppermute | solution.py:227
  11.4 17.7 %collective-permute-start = (bf16[272,512]{1,0:T(8,128)(2,1)S(1)}, bf16[272,512]{1,0:T(8,128)(2,1)S(1)}, u32[]{:S(2)}, u32[]{:S(2)}) collective-permute-start(bf16[272,512]{1,0:T(8,128)(2,1)S(1)} %get-tuple-element.24.far_sent_ref), channel_id=1, source_target_pairs={{1,2},{3,4},{5,6},{7,8},{9,10},{11,12},{13,14},{15,16},{17,18},{19... | collective-permute-start | bytes 835592 | tf_op jit(solution)/shard_map/ppermute | solution.py:226
  14.4 2.3 %copy-start.3 = (bf16[3,3,512,512]{3,2,1,0:T(8,128)(2,1)S(1)}, bf16[3,3,512,512]{3,2,1,0:T(8,128)(2,1)}, u32[]{:S(2)}) copy-start(bf16[3,3,512,512]{3,2,1,0:T(8,128)(2,1)} %conv_hbm) | copy-start | bytes 14155780
  16.8 5.7 %copy-start.4 = (bf16[512,512]{1,0:T(8,128)(2,1)S(1)}, bf16[512,512]{1,0:T(8,128)(2,1)}, u32[]{:S(2)}) copy-start(bf16[512,512]{1,0:T(8,128)(2,1)} %param.14) | copy-start | bytes 1572868
  17.1 2.1 %copy-start = (bf16[3,3,512,512]{3,2,1,0:T(8,128)(2,1)}, bf16[3,3,512,512]{3,2,1,0:T(8,128)(2,1)S(1)}, u32[]{:S(2)}) copy-start(bf16[3,3,512,512]{3,2,1,0:T(8,128)(2,1)S(1)} %fetch.1.conv_ref) | copy-start | bytes 14155780
  19.2 4.3 %collective-permute-start.1 = (bf16[16,2,8,512]{3,2,1,0:T(8,128)(2,1)S(1)}, bf16[16,2,8,512]{3,2,1,0:T(8,128)(2,1)S(1)}, u32[]{:S(2)}, u32[]{:S(2)}) collective-permute-start(bf16[16,2,8,512]{3,2,1,0:T(8,128)(2,1)S(1)} %all-to-all-done.same_ref), channel_id=1, source_target_pairs={{0,1},{1,0},{2,3},{3,2},{4,5},{5,4},{6,7},{7,6},{8,9},{9,8},{10,11... | collective-permute-start | bytes 786440 | tf_op jit(solution)/shard_map/ppermute | solution.py:240
  23.6 2.3 %copy-start.1 = (bf16[3,3,512,512]{3,2,1,0:T(8,128)(2,1)S(1)}, bf16[3,3,512,512]{3,2,1,0:T(8,128)(2,1)}, u32[]{:S(2)}) copy-start(bf16[3,3,512,512]{3,2,1,0:T(8,128)(2,1)} %copy-done) | copy-start | bytes 14155780
  25.9 3.2 %copy-start.2 = (bf16[3,3,512,512]{3,2,1,0:T(8,128)(2,1)S(1)}, bf16[3,3,512,512]{3,2,1,0:T(8,128)(2,1)}, u32[]{:S(2)}) copy-start(bf16[3,3,512,512]{3,2,1,0:T(8,128)(2,1)} %copy-done) | copy-start | bytes 14155780
